TPU v7x, 32 devices: a whole 2x2x4 slice. The times are simulated.
32 devices in a mesh: groups: 2 (over y), ctx: 2 (over x), exp: 8 (over z, core).
Axes of the slice: x: 2, y: 2, z: 4, core: 2. Of those that a mesh axis runs over, the one named last changes fastest.
Arguments:
- resid_in: bfloat16 [512, 3072], P(('groups', 'ctx', 'exp')), parts along dimension 0, may hold values from -6 to 6
- queries: bfloat16 [512, 2048], P(('groups', 'ctx'), 'exp'), parts along dimension 0, may hold values from -1.75 to 1.75
- keys: bfloat16 [512, 2048], P(('groups', 'ctx'), 'exp'), parts along dimension 0, may hold values from -1.75 to 1.75
- values: bfloat16 [512, 2048], P(('groups', 'ctx'), 'exp'), parts along dimension 0, may hold values from -40 to 40
- out_gate: bfloat16 [512, 2048], P(('groups', 'ctx'), 'exp'), parts along dimension 0, may hold values from -8 to 8
- log_decay: float32 [16, 512], P('exp', ('groups', 'ctx')), parts along dimension 1, may hold values from -1 to 0
- attn_gain: float32 [2048], P('exp'), may hold values from 0.1 to 1.9
- out_proj: bfloat16 [2048, 3072], P('exp'), may hold values from -0.125 to 0.125
- moe_gain: float32 [3072], replicated, may hold values from 0.1 to 1.9
- routes: int32 [512, 2], P(('groups', 'ctx', 'exp')), parts along dimension 0, may hold values from 0 to 3, all different within a row; in each aligned block of 16 rows (0 to 15, 16 to 31, ...) at most 12 rows name the same one
- route_weight: float32 [512, 2], P(('groups', 'ctx', 'exp')), parts along dimension 0, may hold values from 0.2 to 1
- w_gate: bfloat16 [8, 3072, 2304], P('exp', None, 'ctx'), may hold values from -0.109375 to 0.109375
- w_up: bfloat16 [8, 3072, 2304], P('exp', None, 'ctx'), may hold values from -0.109375 to 0.109375
- w_down: bfloat16 [8, 2304, 3072], P('exp', None, 'ctx'), may hold values from -0.09375 to 0.09375
Outputs:
- mixed: bfloat16 [512, 3072], P(('groups', 'ctx', 'exp')), parts along dimension 0
There are 2 independent parts, one for each index of `groups`. A program takes and returns all parts, laid end to end along the dimension named above; an argument that names none is the same for every part. Nothing has to cross between parts.
Inputs may be any that keep to these rules, and one draw needn't show every extreme that they name: `routes`: each row names two different experts; in the 16 rows of one device no expert is named more than 12 times, and 12 is reached.
All inputs are finite; a program needn't handle non-finite values.
Results may differ from a plain program's by a relative error of at most 0.006.
Values may be sent and summed in bfloat16 or wider, within the bound.
A program may use at most 128 MiB of HBM per device.

v0:
```python
import jax
import jax.numpy as jnp
from jax import lax
from jax.sharding import PartitionSpec as P

HIGHEST = lax.Precision.HIGHEST


def from_behind(block, axis, distance):
    devices = range(lax.axis_size(axis))
    route = [(i - distance, i) for i in devices if i - distance in devices]
    return lax.ppermute(block, axis, route)


def local_terms(query_block, key_block, value_block, log_rates):
    cumulative = jnp.cumsum(log_rates, axis=1)
    scores = jnp.einsum("thd,shd->hts", query_block, key_block, preferred_element_type=jnp.float32)
    length = log_rates.shape[1]
    later = (
        jnp.arange(length, dtype=jnp.int32)[:, None] >= jnp.arange(length, dtype=jnp.int32)[None, :]
    )
    spread = cumulative[:, :, None] - cumulative[:, None, :]
    weights = jnp.where(later[None], jnp.exp(jnp.minimum(spread, 0.0)), 0.0)
    value_float = value_block.astype(jnp.float32)
    inner_part = jnp.einsum("hts,shd->thd", scores * weights, value_float, precision=HIGHEST)
    tail_decay = jnp.exp(cumulative[:, -1:] - cumulative)
    key_scaled = key_block.astype(jnp.float32) * jnp.transpose(tail_decay)[:, :, None]
    local_state = jnp.einsum("shd,she->hde", key_scaled, value_float, precision=HIGHEST)
    query_scaled = query_block.astype(jnp.float32) * jnp.transpose(jnp.exp(cumulative))[:, :, None]
    return (inner_part, query_scaled, local_state, jnp.exp(cumulative[:, -1]))


def head_gate(attended, out_gate, attn_gain):
    token_count, head_count, head_width = attended.shape
    scale_rows = lax.rsqrt(jnp.mean(attended * attended, axis=-1, keepdims=True) + 1e-06)
    gain_table = attn_gain.reshape(head_count, head_width)
    opening = jax.nn.sigmoid(out_gate.astype(jnp.float32)).reshape(attended.shape)
    gated = opening * attended * scale_rows * gain_table
    return gated.reshape(token_count, head_count * head_width).astype(jnp.bfloat16)


def rms_rows(rows_in, gain):
    values_float = rows_in.astype(jnp.float32)
    scale_rows = lax.rsqrt(jnp.mean(values_float * values_float, axis=-1, keepdims=True) + 1e-06)
    return (values_float * scale_rows * gain).astype(jnp.bfloat16)


def slot_tables(route_rows, expert_count, capacity):
    leading = route_rows.shape[:-2]
    pair_ids = route_rows.reshape(leading + (-1,))
    onehot = (pair_ids[..., None] == jnp.arange(expert_count, dtype=jnp.int32)).astype(jnp.int32)
    earlier = jnp.cumsum(onehot, axis=-2) - onehot
    slot_ids = jnp.sum(earlier * onehot, axis=-1)
    slot_hit = (slot_ids[..., None] == jnp.arange(capacity, dtype=jnp.int32)).astype(jnp.float32)
    expert_hit = onehot.astype(jnp.float32).reshape(route_rows.shape + (expert_count,))
    return (expert_hit, slot_hit.reshape(route_rows.shape + (capacity,)))


def per_device(
    resid_in,
    queries,
    keys,
    values,
    out_gate,
    log_decay,
    attn_gain,
    out_proj,
    moe_gain,
    routes,
    route_weight,
    w_gate,
    w_up,
    w_down,
):
    head_count = log_decay.shape[0]
    token_count = queries.shape[0]
    head_width = queries.shape[1] // head_count
    shaped = (token_count, head_count, head_width)
    inner_part, query_scaled, local_state, block_decay = local_terms(
        queries.reshape(shaped), keys.reshape(shaped), values.reshape(shaped), log_decay
    )
    ctx_size = lax.axis_size("ctx")
    exp_size = lax.axis_size("exp")
    empty_state = jnp.zeros_like(local_state)

    def advance(turn_index, incoming):
        carried = block_decay[:, None, None] * incoming + local_state
        return from_behind(carried, "ctx", 1)

    incoming = lax.fori_loop(0, ctx_size - 1, advance, empty_state)
    attended = inner_part + jnp.einsum("thd,hde->the", query_scaled, incoming, precision=HIGHEST)
    gated = head_gate(attended, out_gate, attn_gain)
    attn_sum = lax.psum_scatter(
        jnp.dot(gated, out_proj, preferred_element_type=jnp.float32),
        "exp",
        scatter_dimension=0,
        tiled=True,
    )
    resid = (resid_in.astype(jnp.float32) + attn_sum).astype(jnp.bfloat16)
    normed = rms_rows(resid, moe_gain)
    row_count = resid.shape[0]
    expert_count = exp_size // 2
    capacity = min(row_count, 6 * token_count // (exp_size * exp_size))
    hit_expert, hit_slot = slot_tables(routes, expert_count, capacity)
    gate_local = w_gate[0]
    up_local = w_up[0]
    down_local = w_down[0]
    all_rows, all_routes = (
        lax.all_gather(normed[None], "ctx", axis=0, tiled=True),
        lax.all_gather(routes[None], "ctx", axis=0, tiled=True),
    )
    every_expert, every_slot = slot_tables(all_routes, expert_count, capacity)
    picker = jnp.repeat(jnp.einsum("crke,crks->cesr", every_expert, every_slot), 2, axis=1).astype(
        jnp.bfloat16
    )
    outgoing = jnp.einsum(
        "cosr,crd->cosd", picker, all_rows, preferred_element_type=jnp.float32
    ).astype(jnp.bfloat16)
    arrived = lax.all_to_all(outgoing, "exp", split_axis=1, concat_axis=1, tiled=True)
    gate_part = jnp.einsum("abcd,dh->abch", arrived, gate_local, preferred_element_type=jnp.float32)
    up_part = jnp.einsum("abcd,dh->abch", arrived, up_local, preferred_element_type=jnp.float32)
    hidden = (jax.nn.silu(gate_part) * up_part).astype(jnp.bfloat16)
    partial_out = jnp.einsum(
        "abch,hn->abcn",
        lax.all_gather(hidden, "ctx", axis=3, tiled=True),
        down_local,
        preferred_element_type=jnp.float32,
    )
    came_back = lax.all_to_all(
        lax.all_to_all(partial_out, "ctx", split_axis=0, concat_axis=3, tiled=True),
        "exp",
        split_axis=1,
        concat_axis=1,
        tiled=True,
    )
    halves = came_back[0].reshape(expert_count, 2, capacity, came_back.shape[-1])
    paired = halves[:, 0] + halves[:, 1]
    mixing = jnp.einsum("rk,rke,rks->res", route_weight, hit_expert, hit_slot)
    moe_sum = jnp.einsum("res,esd->rd", mixing, paired, precision=HIGHEST)
    return (resid.astype(jnp.float32) + moe_sum).astype(jnp.bfloat16)


def solution(mesh):
    return jax.shard_map(
        per_device,
        mesh=mesh,
        in_specs=(
            P(("groups", "ctx", "exp"), None),
            P(("groups", "ctx"), "exp"),
            P(("groups", "ctx"), "exp"),
            P(("groups", "ctx"), "exp"),
            P(("groups", "ctx"), "exp"),
            P("exp", ("groups", "ctx")),
            P("exp"),
            P("exp", None),
            P(),
            P(("groups", "ctx", "exp"), None),
            P(("groups", "ctx", "exp"), None),
            P("exp", None, "ctx"),
            P("exp", None, "ctx"),
            P("exp", None, "ctx"),
        ),
        out_specs=P(("groups", "ctx", "exp"), None),
        check_vma=False,
    )
```

profile of v0, /device:TPU:0, one launch (start us, length us, event | category | flops | bytes accessed | tf_op | source)
XLA Modules:
  0.0 188.1 jit_solution(17238360264318478694)
XLA Ops:
  6.5 0.0 copy-start
  6.5 0.0 reduce-scatter.2.cloned.1.call-start
  6.6 1.1 reduce_window_sum.33
  7.7 0.2 slice_reduce_fusion
  7.9 0.1 exponential_bitcast_fusion
  7.9 1.0 copy.93
  8.9 1.0 convolution_add_fusion
  10.0 4.8 %collective-permute-start = (f32[2,128,128]{2,1,0:T(8,128)S(1)}, f32[2,128,128]{2,1,0:T(8,128)S(1)}, u32[]{:S(2)}, u32[]{:S(2)}) collective-permute-start(f32[2,128,128]{2,1,0:T(8,128)S(1)} %convolution_add_fusion), channel_id=1, source_target_pairs={{0,8},{1,9},{2,10},{3,11},{4,12},{5,13},{6,14},{7,15},{16,24},{17,... | collective-permute-start | bytes 393224 | tf_op jit(solution)/shard_map/while/body/eval_jaxpr/ppermute | solution.py:12
  14.9 0.9 add_divide_fusion
  15.7 0.1 copy.60
  15.8 1.0 convolution_multiply_fusion
  16.8 0.0 copy-done.1
  16.8 0.3 convolution_bitcast_fusion.2
  17.1 0.4 collective-permute-done
  17.6 0.0 copy-done.3
  17.6 0.5 multiply_reduce_fusion
  18.0 0.0 copy-done.6
  18.0 0.1 multiply_convert_fusion
  18.2 0.0 copy-done
  18.2 1.6 fusion.58
  19.7 0.0 reduce-scatter.2.cloned.1.call-update
  19.8 0.6 copy-done.5
  20.4 4.7 %all-gather.2 = s32[2,16,2]{1,2,0:T(2,128)S(1)} all-gather(s32[1,16,2]{1,2,0:T(2,128)S(1)} %bitcast.106), channel_id=2, replica_groups=mesh['groups'=2,'ctx'=2,'exp'=8] {'ctx'}, dimensions={0}, use_global_device_ids=true | all-gather | bytes 384 | tf_op jit(solution)/shard_map/all_gather | solution.py:110
  25.1 0.1 copy.71
  25.2 0.1 eq.87
  25.2 0.1 fusion.44
  25.3 0.1 reduce_window_sum.35
  25.4 0.2 select_reduce_fusion
  25.6 0.1 eq.91
  25.7 0.4 fusion.17
  26.0 0.1 copy.73
  26.2 30.2 %reduce-scatter.2.cloned.1.call-done = f32[16,3072]{1,0:T(8,128)} async-done(((f32[128,3072]{1,0:T(8,128)}), f32[16,3072]{1,0:T(8,128)}) %reduce-scatter.2.cloned.1.call-update) | async-done | bytes 196624 | tf_op jit(solution)/shard_map/reduce_scatter | solution.py:93
  56.4 0.0 copy-done.2
  56.4 1.1 fusion.21
  57.5 0.1 fusion.23
  57.6 5.3 %all-gather.1 = bf16[32,3072]{1,0:T(8,128)(2,1)S(1)} all-gather(bf16[16,3072]{1,0:T(8,128)(2,1)S(1)} %fusion.23), channel_id=3, replica_groups=mesh['groups'=2,'ctx'=2,'exp'=8] {'ctx'}, dimensions={0}, use_global_device_ids=true | all-gather | bytes 294912 | tf_op jit(solution)/shard_map/all_gather | solution.py:109
  62.9 0.5 convolution_convert_fusion
  63.4 1.2 copy.74
  64.6 0.0 slice-start
  64.6 32.1 %all_to_all.28 = bf16[2,8,12,3072]{3,0,2,1:T(2,128)(2,1)S(1)} all-to-all(bf16[2,8,12,3072]{3,0,2,1:T(2,128)(2,1)S(1)} %copy.74), channel_id=1, replica_groups=mesh['groups'=2,'ctx'=2,'exp'=8] {'exp'}, dimensions={1} | all-to-all | bytes 2359296 | tf_op jit(solution)/shard_map/all_to_all | solution.py:119
  96.7 5.4 %fusion.4 = f32[2,8,12,1152]{3,2,1,0:T(8,128)S(1)} fusion(bf16[1,3072,1152]{2,1,0:T(8,128)(2,1)} %param.25, bf16[2,8,12,3072]{3,0,2,1:T(2,128)(2,1)S(1)} %all_to_all.28), kind=kOutput, calls=%fused_computation.4 | convolution fusion | flops 1358954496 | bytes 9142272 | tf_op jit(solution)/shard_map/abcd,dh->abch/dot_general | solution.py:120
  102.1 0.0 slice-start.3
  102.1 2.3 %fusion.11 = bf16[2,8,12,1152]{3,2,1,0:T(8,128)(2,1)S(1)} fusion(bf16[1,3072,1152]{2,1,0:T(8,128)(2,1)S(1)} %bitcast.109, bf16[2,8,12,3072]{3,0,2,1:T(2,128)(2,1)S(1)} %all_to_all.28, f32[2,8,12,1152]{3,2,1,0:T(8,128)S(1)} %fusion.4), kind=kOutput, calls=%fused_computation.11 | convolution fusion | flops 1360281600 | bytes 9584640 | tf_op jit(solution)/shard_map/abcd,dh->abch/dot_general | solution.py:121
  104.4 15.6 %all_gather.11 = bf16[2,8,12,2304]{3,2,1,0:T(8,128)(2,1)S(1)} all-gather(bf16[2,8,12,1152]{3,2,1,0:T(8,128)(2,1)S(1)} %fusion.11), channel_id=1, replica_groups=mesh['groups'=2,'ctx'=2,'exp'=8] {'ctx'}, dimensions={3}, use_global_device_ids=true | all-gather | bytes 1327104 | tf_op jit(solution)/shard_map/all_gather | solution.py:125
  120.0 0.0 slice-done.3
  120.0 1.6 fusion
  121.6 16.7 %all_to_all.29 = f32[2,8,12,1536]{3,1,2,0:T(8,128)S(1)} all-to-all(f32[2,8,12,1536]{3,1,2,0:T(8,128)S(1)} %fusion), channel_id=1, replica_groups=mesh['groups'=2,'ctx'=2,'exp'=8] {'ctx'}, dimensions={0} | all-to-all | bytes 2359296 | tf_op jit(solution)/shard_map/all_to_all | solution.py:130
  138.3 0.9 copy.90
  139.2 2.8 %reshape.100 = f32[1,8,12,3072]{3,0,2,1:T(1,128)} reshape(f32[1,8,12,2,1536]{4,3,2,1,0:T(2,128)S(1)} %copy.90) | data formatting | bytes 2359296 | tf_op jit(solution)/shard_map/all_to_all | solution.py:130
  142.0 3.7 %all-to-all-start.2 = ((f32[1,8,12,3072]{3,0,2,1:T(1,128)}), f32[1,8,12,3072]{3,0,2,1:T(1,128)S(1)}, u32[]{:S(2)}, u32[]{:S(2)}) async-start(f32[1,8,12,3072]{3,0,2,1:T(1,128)} %reshape.100), calls=%async_computation.3 | async-start | bytes 2359296 | tf_op jit(solution)/shard_map/all_to_all | solution.py:129
  145.7 0.1 copy.68
  145.8 0.1 eq.79
  145.9 0.1 fusion.53
  146.0 0.1 reduce_window_sum.34
  146.0 0.2 select_reduce_fusion.1
  146.2 0.1 eq.83
  146.3 0.0 copy-done.7
  146.3 0.1 copy.69
  146.4 0.4 fusion.45
  146.8 28.3 %all-to-all-done.2 = f32[1,8,12,3072]{3,0,2,1:T(1,128)S(1)} async-done(((f32[1,8,12,3072]{3,0,2,1:T(1,128)}), f32[1,8,12,3072]{3,0,2,1:T(1,128)S(1)}, u32[]{:S(2)}, u32[]{:S(2)}) %all-to-all-start.2) | async-done | bytes 1179680 | tf_op jit(solution)/shard_map/all_to_all | solution.py:129
  175.1 1.7 copy.80
  176.7 2.0 %reshape_squeeze.3 = f32[4,2,12,3072]{3,1,0,2:T(2,128)S(1)} reshape(f32[1,8,12,3072]{3,1,2,0:T(8,128)} %copy.80) | data formatting | bytes 2359296 | tf_op jit(solution)/shard_map/reshape;squeeze | solution.py:136
  178.8 0.7 slice_add_fusion
  179.4 1.8 fusion.7
  (20 shorter events, 0.1 us)
Async XLA Ops:
  6.5 11.6 %copy-start = (bf16[256,3072]{1,0:T(8,128)(2,1)S(1)}, bf16[256,3072]{1,0:T(8,128)(2,1)}, u32[]{:S(2)}) copy-start(bf16[256,3072]{1,0:T(8,128)(2,1)} %param.21) | copy-start | bytes 4718596
  6.5 10.3 %copy-start.1 = (bf16[128,256]{1,0:T(8,128)(2,1)S(1)}, bf16[128,256]{1,0:T(8,128)(2,1)}, u32[]{:S(2)}) copy-start(bf16[128,256]{1,0:T(8,128)(2,1)} %param.17) | copy-start | bytes 196612
  6.5 11.0 %copy-start.3 = (bf16[128,256]{1,0:T(8,128)(2,1)S(1)}, bf16[128,256]{1,0:T(8,128)(2,1)}, u32[]{:S(2)}) copy-start(bf16[128,256]{1,0:T(8,128)(2,1)} %param.15) | copy-start | bytes 196612
  6.5 11.5 %copy-start.6 = (f32[256]{0:T(256)S(1)}, f32[256]{0:T(256)}, u32[]{:S(2)}) copy-start(f32[256]{0:T(256)} %param.20) | copy-start | bytes 3076
  6.5 49.8 %reduce-scatter.2.cloned.1.call-start = ((), (), s32[]{:S(2)}) async-start(), calls=%async_computation.4 | async-start | bytes 1769472 | tf_op jit(solution)/shard_map/reduce_scatter | solution.py:93
  10.0 7.6 %collective-permute-start = (f32[2,128,128]{2,1,0:T(8,128)S(1)}, f32[2,128,128]{2,1,0:T(8,128)S(1)}, u32[]{:S(2)}, u32[]{:S(2)}) collective-permute-start(f32[2,128,128]{2,1,0:T(8,128)S(1)} %convolution_add_fusion), channel_id=1, source_target_pairs={{0,8},{1,9},{2,10},{3,11},{4,12},{5,13},{6,14},{7,15},{16,24},{17,... | collective-permute-start | bytes 393224 | tf_op jit(solution)/shard_map/while/body/eval_jaxpr/ppermute | solution.py:12
  19.7 0.7 copy-start.5
  19.7 36.6 %copy-start.2 = (bf16[16,3072]{1,0:T(8,128)(2,1)S(1)}, bf16[16,3072]{1,0:T(8,128)(2,1)}, u32[]{:S(2)}) copy-start(bf16[16,3072]{1,0:T(8,128)(2,1)} %param.14) | copy-start | bytes 294916
  19.7 37.7 %copy-start.4 = (f32[3072]{0:T(1024)S(1)}, f32[3072]{0:T(1024)}, u32[]{:S(2)}) copy-start(f32[3072]{0:T(1024)} %param.22) | copy-start | bytes 36868
  64.6 37.5 %slice-start = ((s8[7077888]{0:T(1024)(128)(4,1)}), s8[2883584]{0:T(1024)(128)(4,1)S(1)}, s32[]{:S(2)}) async-start(s8[7077888]{0:T(1024)(128)(4,1)} %bitcast.108), calls=%async_computation.5 | async-start | bytes 5767168
  96.7 5.4 %slice-start.1 = ((s8[7077888]{0:T(1024)(128)(4,1)}), s8[4194304]{0:T(1024)(128)(4,1)S(1)}, s32[]{:S(2)}) async-start(s8[7077888]{0:T(1024)(128)(4,1)} %bitcast.108), calls=%async_computation.6 | async-start | bytes 8388608
  96.7 23.3 %slice-start.2 = ((s8[7077888]{0:T(1024)(128)(4,1)}), s8[4194304]{0:T(1024)(128)(4,1)S(1)}, s32[]{:S(2)}) async-start(s8[7077888]{0:T(1024)(128)(4,1)} %bitcast.110), calls=%async_computation.7 | async-start | bytes 8388608
  102.1 17.9 %slice-start.3 = ((s8[7077888]{0:T(1024)(128)(4,1)}), s8[2883584]{0:T(1024)(128)(4,1)S(1)}, s32[]{:S(2)}) async-start(s8[7077888]{0:T(1024)(128)(4,1)} %bitcast.110), calls=%async_computation.8 | async-start | bytes 5767168
  142.0 4.3 %copy-start.7 = (f32[16,2]{0,1:T(2,128)S(1)}, f32[16,2]{0,1:T(2,128)}, u32[]{:S(2)}) copy-start(f32[16,2]{0,1:T(2,128)} %param.24) | copy-start | bytes 388
  142.0 33.0 %all-to-all-start.2 = ((f32[1,8,12,3072]{3,0,2,1:T(1,128)}), f32[1,8,12,3072]{3,0,2,1:T(1,128)S(1)}, u32[]{:S(2)}, u32[]{:S(2)}) async-start(f32[1,8,12,3072]{3,0,2,1:T(1,128)} %reshape.100), calls=%async_computation.3 | async-start | bytes 2359296 | tf_op jit(solution)/shard_map/all_to_all | solution.py:129
Sparse Core Ops, SparseCore 0:
  19.9 36.4 reduce-scatter.1
where the time goes:
time: 189 us; the launch traced here: 188 us
  blocking collectives  74.2 us (39%)
  waiting for transfers between devices  58.9 us (31%)
  matrix products  16.8 us (9%)
  between operations  13.6 us (7%)
  local copies, waits for them, and re-layouts  11.3 us (6%)
  starting transfers between devices  8.58 us (5%)
  other arithmetic  4.64 us (2%)
    all_to_all x1, blocking collectives, per_device(): lax.all_to_all(outgoing, 'exp', split_axis=1, concat_axis=1, tiled=True)  32.1 us
    reduce_scatter x1, waiting for transfers between devices, per_device(): lax.psum_scatter(jnp.dot(gated, out_proj, preferred_element_type=jnp.floa...  30.2 us
    all_to_all x1, waiting for transfers between devices, per_device(): lax.all_to_all(lax.all_to_all(partial_out, 'ctx', split_axis=0, concat_ax...  28.3 us
    all_to_all x1, blocking collectives, per_device(): lax.all_to_all(partial_out, 'ctx', split_axis=0, concat_axis=3, tiled=True)  16.7 us
    all_gather x1, blocking collectives, per_device(): lax.all_gather(hidden, 'ctx', axis=3, tiled=True)  15.6 us
    dot_general x1, matrix products, per_device(): jnp.einsum('abcd,dh->abch', arrived, gate_local, preferred_element_type=j...  5.37 us
    all_gather x1, blocking collectives, per_device(): lax.all_gather(normed[None], 'ctx', axis=0, tiled=True)  5.29 us
    ppermute x1, starting transfers between devices, from_behind(): return lax.ppermute(block, axis, route)  4.85 us
  transfers between devices with their start and end apart: 3, of which 3 were waited for; matrix products, arithmetic and copies ran while one was open for 2% of the time, Pallas kernels for 0%

commit v1 on v0

--- a/solution.py
+++ b/solution.py
@@ -1,6 +1,10 @@
+import functools
+
 import jax
 import jax.numpy as jnp
 from jax import lax
+from jax.experimental import pallas as pl
+from jax.experimental.pallas import tpu as pltpu
 from jax.sharding import PartitionSpec as P
 
 HIGHEST = lax.Precision.HIGHEST
@@ -140,9 +144,512 @@
     return (resid.astype(jnp.float32) + moe_sum).astype(jnp.bfloat16)
 
 
+MESH = pl.DeviceIdType.MESH
+PROJ_TILES = 3
+WIDE = 256
+
+
+def dot32(left, right):
+    return jnp.dot(left, right, preferred_element_type=jnp.float32)
+
+
+def layer_kernel(
+    zs,
+    capacity,
+    resid_in,
+    queries,
+    keys,
+    values,
+    out_gate,
+    log_decay,
+    attn_gain,
+    out_proj_hbm,
+    moe_gain,
+    routes,
+    route_weight,
+    w_gate_hbm,
+    w_up_hbm,
+    w_down_hbm,
+    mixed,
+    out_proj,
+    w_gate,
+    w_up,
+    w_rest,
+    w_down,
+    info,
+    state_out,
+    state_in,
+    gated,
+    pair_out,
+    pair_in,
+    proj_out,
+    proj_in,
+    resid,
+    rows_in,
+    picked,
+    hidden_own,
+    hidden_in,
+    expert_sum,
+    half_out,
+    half_in,
+    back_out,
+    back_in,
+    last_out,
+    last_in,
+    load_sem,
+    info_send,
+    info_recv,
+    one_send,
+    one_recv,
+    pair_send,
+    pair_recv,
+    proj_send,
+    proj_recv,
+    gather_send,
+    gather_recv,
+    hidden_send,
+    hidden_recv,
+    half_send,
+    half_recv,
+    back_send,
+    back_recv,
+):
+    ctx = lax.axis_index("ctx")
+    exp = lax.axis_index("exp")
+    core = lax.rem(exp, 2)
+    level = exp // 2
+    row_count, width = resid_in.shape
+    tokens = queries.shape[0]
+    heads = log_decay.shape[0]
+    head_width = queries.shape[1] // heads
+    half = w_gate_hbm.shape[2]
+    whole = half // WIDE * WIDE
+    rest = half - whole
+    columns = w_down_hbm.shape[2]
+    cap_rows = zs * capacity
+    tile = width // PROJ_TILES
+    other_ctx = 1 - ctx
+
+    def ahead(d):
+        return lax.rem(level + d, zs)
+
+    def behind(d):
+        return lax.rem(level + zs - d, zs)
+
+    def device(at_ctx, at_level, at_core):
+        return {"ctx": at_ctx, "exp": at_level * 2 + at_core}
+
+    core_partner = device(ctx, level, 1 - core)
+    ctx_partner = device(other_ctx, level, core)
+
+    loads = [
+        pltpu.make_async_copy(out_proj_hbm, out_proj, load_sem.at[0]),
+        pltpu.make_async_copy(w_gate_hbm.at[0, :, pl.ds(0, whole)], w_gate, load_sem.at[1]),
+        pltpu.make_async_copy(w_up_hbm.at[0, :, pl.ds(0, whole)], w_up, load_sem.at[2]),
+        pltpu.make_async_copy(
+            w_gate_hbm.at[0, :, pl.ds(whole, rest)], w_rest.at[:, pl.ds(0, rest)], load_sem.at[3]
+        ),
+        pltpu.make_async_copy(
+            w_up_hbm.at[0, :, pl.ds(whole, rest)], w_rest.at[:, pl.ds(rest, rest)], load_sem.at[4]
+        ),
+        pltpu.make_async_copy(w_down_hbm.at[0], w_down, load_sem.at[5]),
+    ]
+    for load in loads:
+        load.start()
+
+    barrier = pltpu.get_barrier_semaphore()
+    peers = [core_partner, ctx_partner]
+    for d in range(1, zs):
+        peers.append(device(ctx, ahead(d), core))
+        peers.append(device(other_ctx, ahead(d), core))
+    for peer in peers:
+        pl.semaphore_signal(barrier, inc=1, device_id=peer, device_id_type=MESH)
+
+    def send(source, target, send_sem, recv_sem, peer):
+        copy = pltpu.make_async_remote_copy(
+            src_ref=source,
+            dst_ref=target,
+            send_sem=send_sem,
+            recv_sem=recv_sem,
+            device_id=peer,
+            device_id_type=MESH,
+        )
+        copy.start()
+        return copy
+
+    sent = []
+    lane = lax.broadcasted_iota(jnp.int32, (row_count, 128), 1)
+    own_routes = routes[...].astype(jnp.float32)
+    own_weight = route_weight[...]
+    info[0, 0] = jnp.where(
+        lane == 0,
+        own_routes[:, 0:1],
+        jnp.where(
+            lane == 1,
+            own_routes[:, 1:2],
+            jnp.where(lane == 2, own_weight[:, 0:1], own_weight[:, 1:2]),
+        ),
+    )
+
+    later_row = lax.broadcasted_iota(jnp.int32, (tokens, tokens), 0)
+    later_col = lax.broadcasted_iota(jnp.int32, (tokens, tokens), 1)
+    causal = later_row >= later_col
+    sums = []
+    for h in range(heads):
+        span = pl.ds(h * head_width, head_width)
+        spread = jnp.broadcast_to(log_decay[h : h + 1, :], (tokens, tokens))
+        upright = jnp.transpose(spread)
+        cum_col = jnp.sum(jnp.where(causal, spread, 0.0), axis=1, keepdims=True)
+        cum_row = jnp.sum(jnp.where(later_row <= later_col, upright, 0.0), axis=0, keepdims=True)
+        sums.append((cum_col, cum_row))
+        tail = jnp.exp(cum_row[:, tokens - 1 : tokens] - cum_row)
+        key_up = jnp.transpose(keys[:, span].astype(jnp.float32)) * tail
+        state_out[h] = dot32(key_up.astype(jnp.bfloat16), values[:, span]).astype(jnp.bfloat16)
+
+    pl.semaphore_wait(barrier, len(peers))
+    state_copy = send(state_out, state_in, one_send.at[0], one_recv.at[0], ctx_partner)
+    infos = []
+    for rel in range(2):
+        for d in range(zs):
+            if rel or d:
+                infos.append(
+                    send(
+                        info.at[0, 0],
+                        info.at[rel, d],
+                        info_send.at[rel * zs + d],
+                        info_recv.at[rel * zs + d],
+                        device(other_ctx if rel else ctx, ahead(d), core),
+                    )
+                )
+    inner = []
+    for h in range(heads):
+        span = pl.ds(h * head_width, head_width)
+        cum_col, cum_row = sums[h]
+        scores = lax.dot_general(
+            queries[:, span],
+            keys[:, span],
+            (((1,), (1,)), ((), ())),
+            preferred_element_type=jnp.float32,
+        )
+        decay = jnp.where(causal, jnp.exp(jnp.minimum(cum_col - cum_row, 0.0)), 0.0)
+        inner.append(dot32((scores * decay).astype(jnp.bfloat16), values[:, span]))
+    state_copy.wait_recv()
+    for h in range(heads):
+        span = pl.ds(h * head_width, head_width)
+        earlier = dot32(queries[:, span], state_in[h]) * jnp.exp(sums[h][0])
+        attended = inner[h] + jnp.where(ctx == 0, 0.0, earlier)
+        scale = lax.rsqrt(jnp.mean(attended * attended, axis=-1, keepdims=True) + 1e-06)
+        opening = jax.nn.sigmoid(out_gate[:, span].astype(jnp.float32))
+        gated[:, span] = (opening * attended * scale * attn_gain[:, span]).astype(jnp.bfloat16)
+
+    order = [
+        gated[pl.ds(pl.multiple_of(2 * row_count * ahead(d) + row_count * side, row_count), row_count), :]
+        for side in (1 - core, core)
+        for d in range(zs)
+    ]
+    ordered = jnp.concatenate(order, axis=0)
+    loads[0].wait()
+    split = zs * row_count
+    pairs = []
+    mine = []
+    for n in range(PROJ_TILES):
+        product = dot32(ordered, out_proj[:, n * tile : (n + 1) * tile])
+        pair_out[n] = product[:split].astype(jnp.bfloat16)
+        pairs.append(send(pair_out.at[n], pair_in.at[n], pair_send.at[n], pair_recv.at[n], core_partner))
+        mine.append(product[split:])
+    projected = []
+    for n in range(PROJ_TILES):
+        pairs[n].wait_recv()
+        total = mine[n] + pair_in[n].astype(jnp.float32)
+        for d in range(1, zs):
+            proj_out[n, d] = total[d * row_count : (d + 1) * row_count].astype(jnp.bfloat16)
+            projected.append(
+                send(
+                    proj_out.at[n, d],
+                    proj_in.at[n, d],
+                    proj_send.at[n * zs + d],
+                    proj_recv.at[n * zs + d],
+                    device(ctx, ahead(d), core),
+                )
+            )
+        part = slice(n * tile, (n + 1) * tile)
+        resid[:, part] = resid_in[:, part].astype(jnp.float32) + total[:row_count]
+
+    for copy in infos:
+        copy.wait_recv()
+    block = row_count
+    routed = info[...].reshape(2 * zs * block, 128)
+    routed_up = jnp.transpose(routed)
+    mark = level.astype(jnp.float32)
+    count = 2 * zs * block
+    place_row = lax.broadcasted_iota(jnp.int32, (count, count), 0)
+    place_col = lax.broadcasted_iota(jnp.int32, (count, count), 1)
+    same = place_row // block == place_col // block
+    hit_col = jnp.where((routed[:, 0:1] == mark) | (routed[:, 1:2] == mark), 1.0, 0.0)
+    hit_row = jnp.where((routed_up[0:1] == mark) | (routed_up[1:2] == mark), 1.0, 0.0)
+    slot_row = jnp.sum(
+        jnp.where(same & (place_row < place_col), hit_col, 0.0), axis=0, keepdims=True
+    ).astype(jnp.int32)
+    slot_col = jnp.sum(
+        jnp.where(same & (place_col < place_row), hit_row, 0.0), axis=1, keepdims=True
+    ).astype(jnp.int32)
+    index_row = lax.broadcasted_iota(jnp.int32, (1, count), 1) // block * capacity + slot_row
+    index_col = lax.broadcasted_iota(jnp.int32, (count, 1), 0) // block * capacity + slot_col
+    reach_rows = lax.broadcasted_iota(jnp.int32, (cap_rows, count), 0)
+    picker = jnp.where((reach_rows == index_row) & (hit_row > 0.5), 1.0, 0.0).astype(jnp.bfloat16)
+    reach_cols = lax.broadcasted_iota(jnp.int32, (count, 2 * cap_rows), 1)
+    placer = jnp.where((reach_cols == index_col) & (hit_col > 0.5), 1.0, 0.0).astype(jnp.bfloat16)
+
+    for n in range(PROJ_TILES):
+        part = slice(n * tile, (n + 1) * tile)
+        for d in range(1, zs):
+            projected[n * (zs - 1) + d - 1].wait_recv()
+            resid[:, part] += proj_in[n, d].astype(jnp.float32)
+    settled = resid[...].astype(jnp.bfloat16).astype(jnp.float32)
+    resid[...] = settled
+    scale = lax.rsqrt(jnp.mean(settled * settled, axis=-1, keepdims=True) + 1e-06)
+    rows_in[0] = (settled * scale * moe_gain[...]).astype(jnp.bfloat16)
+    gathers = [
+        send(
+            rows_in.at[0],
+            rows_in.at[d],
+            gather_send.at[d],
+            gather_recv.at[d],
+            device(ctx, ahead(d), core),
+        )
+        for d in range(1, zs)
+    ]
+    for copy in gathers:
+        copy.wait_recv()
+    picked[0, 0] = dot32(
+        picker[:, : zs * block], rows_in[...].reshape(zs * block, width)
+    ).astype(jnp.bfloat16)
+    to_ctx = send(picked.at[0, 0], picked.at[1, 0], one_send.at[1], one_recv.at[1], ctx_partner)
+    to_core = send(picked.at[0, 0], picked.at[0, 1], one_send.at[2], one_recv.at[2], core_partner)
+    sent += [to_ctx, to_core]
+    to_core.wait_recv()
+
+    def activate(gate_part, up_part):
+        return (jax.nn.silu(gate_part) * up_part).astype(jnp.bfloat16)
+
+    def hide(rel):
+        def step(n, carry):
+            span = pl.ds(pl.multiple_of(n * WIDE, WIDE), WIDE)
+            rows = picked[rel].reshape(2 * cap_rows, width)
+            hidden_own[rel, :, span] = activate(
+                dot32(rows, w_gate[:, span]), dot32(rows, w_up[:, span])
+            )
+            return carry
+
+        lax.fori_loop(0, whole // WIDE, step, 0)
+        both = dot32(picked[rel].reshape(2 * cap_rows, width), w_rest[...])
+        hidden_own[rel, :, whole:] = activate(both[:, :rest], both[:, rest:])
+        return send(
+            hidden_own.at[rel],
+            hidden_in.at[1 - rel],
+            hidden_send.at[rel],
+            hidden_recv.at[1 - rel],
+            ctx_partner,
+        )
+
+    def lower(rel, first):
+        source = hidden_own if first else hidden_in
+        side = ctx if first else other_ctx
+
+        def step(n, carry):
+            span = pl.ds(pl.multiple_of(n * WIDE, WIDE), WIDE)
+            product = dot32(
+                source[rel], w_down[pl.ds(pl.multiple_of(side * half, 128), half), span]
+            )
+            if first:
+                expert_sum[rel, :, span] = product
+            else:
+                expert_sum[rel, :, span] += product
+            return carry
+
+        lax.fori_loop(0, columns // WIDE, step, 0)
+
+    for load in loads[1:5]:
+        load.wait()
+    hidden_near = hide(0)
+    to_ctx.wait_recv()
+    passed = send(picked.at[1, 0], picked.at[1, 1], one_send.at[3], one_recv.at[3], core_partner)
+    passed.wait_recv()
+    hidden_far = hide(1)
+    loads[5].wait()
+    lower(0, True)
+    lower(1, True)
+
+    def incoming_hidden(rel):
+        return pltpu.make_async_remote_copy(
+            src_ref=hidden_own.at[1 - rel],
+            dst_ref=hidden_in.at[rel],
+            send_sem=hidden_send.at[1 - rel],
+            recv_sem=hidden_recv.at[rel],
+            device_id=ctx_partner,
+            device_id_type=MESH,
+        )
+
+    halves = [None, None]
+    for rel in (1, 0):
+        incoming_hidden(rel).wait_recv()
+        lower(rel, False)
+        half_out[rel] = expert_sum[rel, cap_rows:, :].astype(jnp.bfloat16)
+        halves[rel] = send(
+            half_out.at[rel], half_in.at[rel], half_send.at[rel], half_recv.at[rel], core_partner
+        )
+    backs = {}
+    for rel in (1, 0):
+        halves[rel].wait_recv()
+        total = (expert_sum[rel, :cap_rows, :] + half_in[rel].astype(jnp.float32)).astype(jnp.bfloat16)
+        chosen = placer[rel * zs * block : (rel + 1) * zs * block, rel * cap_rows : (rel + 1) * cap_rows]
+        spread_rows = dot32(chosen, total).astype(jnp.bfloat16)
+        back_in[rel, 0] = spread_rows[:block]
+        for d in range(1, zs):
+            back_out[rel, d] = spread_rows[d * block : (d + 1) * block]
+            backs[rel, d] = send(
+                back_out.at[rel, d],
+                back_in.at[rel, d],
+                back_send.at[rel * zs + d],
+                back_recv.at[rel * zs + d],
+                device(ctx, behind(d), core),
+            )
+
+    def mix(rel):
+        table = info[rel, 0]
+        total = jnp.zeros((block, columns), jnp.float32)
+        for d in range(zs):
+            if d:
+                backs[rel, d].wait_recv()
+            expert = ahead(d).astype(jnp.float32)
+            weight = jnp.where(table[:, 0:1] == expert, table[:, 2:3], 0.0) + jnp.where(
+                table[:, 1:2] == expert, table[:, 3:4], 0.0
+            )
+            total = total + weight * back_in[rel, d].astype(jnp.float32)
+        return total
+
+    last_out[...] = mix(1).astype(jnp.bfloat16)
+    last = send(last_out, last_in, one_send.at[4], one_recv.at[4], ctx_partner)
+    near = pl.ds(pl.multiple_of(ctx * columns, 128), columns)
+    far = pl.ds(pl.multiple_of(other_ctx * columns, 128), columns)
+    mixed[:, near] = (resid[:, near] + mix(0)).astype(jnp.bfloat16)
+    last.wait_recv()
+    mixed[:, far] = (resid[:, far] + last_in[...].astype(jnp.float32)).astype(jnp.bfloat16)
+
+    sent += [state_copy, hidden_near, hidden_far, passed, last]
+    for copy in sent + infos + pairs + projected + gathers + halves + list(backs.values()):
+        copy.wait_send()
+
+
+def per_device_kernel(
+    resid_in,
+    queries,
+    keys,
+    values,
+    out_gate,
+    log_decay,
+    attn_gain,
+    out_proj,
+    moe_gain,
+    routes,
+    route_weight,
+    w_gate,
+    w_up,
+    w_down,
+):
+    zs = lax.axis_size("exp") // 2
+    row_count, width = resid_in.shape
+    tokens = queries.shape[0]
+    heads = log_decay.shape[0]
+    head_width = queries.shape[1] // heads
+    capacity = min(row_count, 6 * tokens // (4 * zs * zs))
+    cap_rows = zs * capacity
+    half = w_gate.shape[2]
+    whole = half // WIDE * WIDE
+    rest = half - whole
+    columns = w_down.shape[2]
+    tile = width // PROJ_TILES
+    low = jnp.bfloat16
+    dma = pltpu.SemaphoreType.DMA
+    vmem = pl.BlockSpec(memory_space=pltpu.VMEM)
+    away = pl.BlockSpec(memory_space=pl.ANY)
+    return pl.pallas_call(
+        functools.partial(layer_kernel, zs, capacity),
+        out_shape=jax.ShapeDtypeStruct((row_count, width), low),
+        in_specs=[vmem] * 7 + [away] + [vmem] * 3 + [away] * 3,
+        out_specs=vmem,
+        scratch_shapes=[
+            pltpu.VMEM(out_proj.shape, low),
+            pltpu.VMEM((width, whole), low),
+            pltpu.VMEM((width, whole), low),
+            pltpu.VMEM((width, 2 * rest), low),
+            pltpu.VMEM(w_down.shape[1:], low),
+            pltpu.VMEM((2, zs, row_count, 128), jnp.float32),
+            pltpu.VMEM((heads, head_width, head_width), low),
+            pltpu.VMEM((heads, head_width, head_width), low),
+            pltpu.VMEM(queries.shape, low),
+            pltpu.VMEM((PROJ_TILES, zs * row_count, tile), low),
+            pltpu.VMEM((PROJ_TILES, zs * row_count, tile), low),
+            pltpu.VMEM((PROJ_TILES, zs, row_count, tile), low),
+            pltpu.VMEM((PROJ_TILES, zs, row_count, tile), low),
+            pltpu.VMEM((row_count, width), jnp.float32),
+            pltpu.VMEM((zs, row_count, width), low),
+            pltpu.VMEM((2, 2, cap_rows, width), low),
+            pltpu.VMEM((2, 2 * cap_rows, half), low),
+            pltpu.VMEM((2, 2 * cap_rows, half), low),
+            pltpu.VMEM((2, 2 * cap_rows, columns), jnp.float32),
+            pltpu.VMEM((2, cap_rows, columns), low),
+            pltpu.VMEM((2, cap_rows, columns), low),
+            pltpu.VMEM((2, zs, row_count, columns), low),
+            pltpu.VMEM((2, zs, row_count, columns), low),
+            pltpu.VMEM((row_count, columns), low),
+            pltpu.VMEM((row_count, columns), low),
+            dma((6,)),
+            dma((2 * zs,)),
+            dma((2 * zs,)),
+            dma((5,)),
+            dma((5,)),
+            dma((PROJ_TILES,)),
+            dma((PROJ_TILES,)),
+            dma((PROJ_TILES * zs,)),
+            dma((PROJ_TILES * zs,)),
+            dma((zs,)),
+            dma((zs,)),
+            dma((2,)),
+            dma((2,)),
+            dma((2,)),
+            dma((2,)),
+            dma((2 * zs,)),
+            dma((2 * zs,)),
+        ],
+        compiler_params=pltpu.CompilerParams(
+            collective_id=0, has_side_effects=True, vmem_limit_bytes=56 * 1024 * 1024
+        ),
+        cost_estimate=pl.CostEstimate(
+            flops=12 * cap_rows * width * half * 2, bytes_accessed=6 * width * half, transcendentals=0
+        ),
+    )(
+        resid_in,
+        queries,
+        keys,
+        values,
+        out_gate,
+        log_decay,
+        attn_gain.reshape(1, -1),
+        out_proj,
+        moe_gain.reshape(1, -1),
+        routes,
+        route_weight,
+        w_gate,
+        w_up,
+        w_down,
+    )
+
+
 def solution(mesh):
+    pairs_of_two = mesh.shape["ctx"] == 2 and mesh.shape["exp"] % 2 == 0
     return jax.shard_map(
-        per_device,
+        per_device_kernel if pairs_of_two else per_device,
         mesh=mesh,
         in_specs=(
             P(("groups", "ctx", "exp"), None),

time: 189 us -> 68.5 us (0.36)
  blocking collectives: 74.2 us -> 0 us
  Pallas kernels: 0 us -> 64.1 us
  waiting for transfers between devices: 58.9 us -> 0 us
  matrix products: 16.8 us -> 0 us
  between operations: 13.6 us -> 0.01 us
  starting transfers between devices: 8.58 us -> 0 us
  local copies, waits for them, and re-layouts: 11.3 us -> 4.24 us
  other arithmetic: 4.64 us -> 0 us
    pallas_call x0 -> x1, Pallas kernels: none -> 64.1 us  [per_device_kernel(): pl.pallas_call(functools.partial(layer_kernel, zs, capacity), out_shape=j...]
    all_to_all x2 -> x0, blocking collectives: 48.7 us -> none  [the longest x1 32.1 us: per_device(): lax.all_to_all(outgoing, 'exp', split_axis=1, concat_axis=1, tiled=True)]
    reduce_scatter x1 -> x0, waiting for transfers between devices: 30.2 us -> none  [per_device(): lax.psum_scatter(jnp.dot(gated, out_proj, preferred_element_type=jnp.floa...]
    all_to_all x1 -> x0, waiting for transfers between devices: 28.3 us -> none  [per_device(): lax.all_to_all(lax.all_to_all(partial_out, 'ctx', split_axis=0, concat_ax...]
    all_gather x3 -> x0, blocking collectives: 25.5 us -> none  [the longest x1 15.6 us: per_device(): lax.all_gather(hidden, 'ctx', axis=3, tiled=True)]
    dot_general x12 -> x0, matrix products: 16.8 us -> none  [the longest x1 5.37 us: per_device(): jnp.einsum('abcd,dh->abch', arrived, gate_local, preferred_element_type=j...]
    all_to_all x3 -> x0, local copies, waits for them, and re-layouts: 5.43 us -> none  [the longest x2 3.74 us: per_device(): lax.all_to_all(partial_out, 'ctx', split_axis=0, concat_axis=3, tiled=True)]
    ppermute x1 -> x0, starting transfers between devices: 4.85 us -> none  [from_behind(): return lax.ppermute(block, axis, route)]
  transfers between devices with their start and end apart: 3 -> 0, of which waited for: 3 -> 0; matrix products, arithmetic and copies ran while one was open for 2% -> 0% of each run, Pallas kernels for 0% -> 0%
where the time goes in v1:
time: 68.5 us; the launch traced here: 68.3 us
  Pallas kernels  64.1 us (94%)
  local copies, waits for them, and re-layouts  4.24 us (6%)
    pallas_call x1, Pallas kernels, per_device_kernel(): pl.pallas_call(functools.partial(layer_kernel, zs, capacity), out_shape=j...  64.1 us
    unnamed x3, local copies, waits for them, and re-layouts  4.24 us

profile of v1, /device:TPU:0, one launch (start us, length us, event | category | flops | bytes accessed | tf_op | source)
XLA Modules:
  0.0 68.3 jit_solution(5785148348237537298)
XLA Ops:
  0.0 1.4 %copy.15.routes = s32[16,2]{1,0:T(8,128)} copy(s32[16,2]{0,1:T(2,128)} %param.23) | data formatting | bytes 256 | tf_op args[9]
  1.4 1.3 %copy.16.route_weight = f32[16,2]{1,0:T(8,128)} copy(f32[16,2]{0,1:T(2,128)} %param.24) | data formatting | bytes 256 | tf_op args[10]
  2.7 64.1 %shard_map.136 = bf16[16,3072]{1,0:T(8,128)(2,1)} custom-call(bf16[16,3072]{1,0:T(8,128)(2,1)} %resid_in.1, bf16[128,256]{1,0:T(8,128)(2,1)} %queries.1, bf16[128,256]{1,0:T(8,128)(2,1)} %keys.1, bf16[128,256]{1,0:T(8,128)(2,1)} %values.1, bf16[128,256]{1,0:T(8,128)(2,1)} %out_gate.1, f32[2,128]{1,0:T(2,128)} %log_decay.1, f32[1,256]{1,0:T(1,128)} %bitcast.3, ...), custom_call_target="tpu_custom_call" | custom-call | flops 4076863488 | bytes 21233664 | tf_op jit(solution)/shard_map/pallas_call | solution.py:576
  66.8 1.5 %copy.18 = bf16[16,3072]{1,0:T(8,128)(2,1)} copy(bf16[16,3072]{1,0:T(8,128)(2,1)} %shard_map.136) | data formatting | bytes 196608

commit v2 on v1

--- a/solution.py
+++ b/solution.py
@@ -207,6 +207,12 @@
     proj_recv,
     gather_send,
     gather_recv,
+    ctx_send,
+    ctx_recv,
+    core_send,
+    core_recv,
+    pass_send,
+    pass_recv,
     hidden_send,
     hidden_recv,
     half_send,
@@ -279,16 +285,22 @@
 
     sent = []
     lane = lax.broadcasted_iota(jnp.int32, (row_count, 128), 1)
-    own_routes = routes[...].astype(jnp.float32)
-    own_weight = route_weight[...]
+    diagonal = lax.broadcasted_iota(jnp.int32, (row_count, row_count), 0) == lax.broadcasted_iota(
+        jnp.int32, (row_count, row_count), 1
+    )
+
+    def upright_pair(flat):
+        return [
+            jnp.sum(jnp.where(diagonal, flat[k : k + 1, :], 0.0), axis=1, keepdims=True)
+            for k in range(2)
+        ]
+
+    own_routes = upright_pair(routes[...].astype(jnp.float32))
+    own_weight = upright_pair(route_weight[...])
     info[0, 0] = jnp.where(
         lane == 0,
-        own_routes[:, 0:1],
-        jnp.where(
-            lane == 1,
-            own_routes[:, 1:2],
-            jnp.where(lane == 2, own_weight[:, 0:1], own_weight[:, 1:2]),
-        ),
+        own_routes[0],
+        jnp.where(lane == 1, own_routes[1], jnp.where(lane == 2, own_weight[0], own_weight[1])),
     )
 
     later_row = lax.broadcasted_iota(jnp.int32, (tokens, tokens), 0)
@@ -409,25 +421,53 @@
     resid[...] = settled
     scale = lax.rsqrt(jnp.mean(settled * settled, axis=-1, keepdims=True) + 1e-06)
     rows_in[0] = (settled * scale * moe_gain[...]).astype(jnp.bfloat16)
+
+    def cut(n):
+        return pl.ds(n * tile, tile)
+
     gathers = [
-        send(
-            rows_in.at[0],
-            rows_in.at[d],
-            gather_send.at[d],
-            gather_recv.at[d],
-            device(ctx, ahead(d), core),
+        [
+            send(
+                rows_in.at[0, :, cut(n)],
+                rows_in.at[d, :, cut(n)],
+                gather_send.at[n * zs + d],
+                gather_recv.at[n * zs + d],
+                device(ctx, ahead(d), core),
+            )
+            for d in range(1, zs)
+        ]
+        for n in range(PROJ_TILES)
+    ]
+    to_ctx, to_core, passed = [], [], []
+
+    def pass_on(n):
+        to_ctx[n].wait_recv()
+        passed.append(
+            send(
+                picked.at[1, 0, :, cut(n)],
+                picked.at[1, 1, :, cut(n)],
+                pass_send.at[n],
+                pass_recv.at[n],
+                core_partner,
+            )
         )
-        for d in range(1, zs)
-    ]
-    for copy in gathers:
+
+    for n in range(PROJ_TILES):
+        for copy in gathers[n]:
+            copy.wait_recv()
+        landed = rows_in[:, :, n * tile : (n + 1) * tile].reshape(zs * block, tile)
+        picked[0, 0, :, cut(n)] = dot32(picker[:, : zs * block], landed).astype(jnp.bfloat16)
+        source = picked.at[0, 0, :, cut(n)]
+        to_ctx.append(
+            send(source, picked.at[1, 0, :, cut(n)], ctx_send.at[n], ctx_recv.at[n], ctx_partner)
+        )
+        to_core.append(
+            send(source, picked.at[0, 1, :, cut(n)], core_send.at[n], core_recv.at[n], core_partner)
+        )
+    for n in range(PROJ_TILES - 1):
+        pass_on(n)
+    for copy in to_core:
         copy.wait_recv()
-    picked[0, 0] = dot32(
-        picker[:, : zs * block], rows_in[...].reshape(zs * block, width)
-    ).astype(jnp.bfloat16)
-    to_ctx = send(picked.at[0, 0], picked.at[1, 0], one_send.at[1], one_recv.at[1], ctx_partner)
-    to_core = send(picked.at[0, 0], picked.at[0, 1], one_send.at[2], one_recv.at[2], core_partner)
-    sent += [to_ctx, to_core]
-    to_core.wait_recv()
 
     def activate(gate_part, up_part):
         return (jax.nn.silu(gate_part) * up_part).astype(jnp.bfloat16)
@@ -472,9 +512,9 @@
     for load in loads[1:5]:
         load.wait()
     hidden_near = hide(0)
-    to_ctx.wait_recv()
-    passed = send(picked.at[1, 0], picked.at[1, 1], one_send.at[3], one_recv.at[3], core_partner)
-    passed.wait_recv()
+    pass_on(PROJ_TILES - 1)
+    for copy in passed:
+        copy.wait_recv()
     hidden_far = hide(1)
     loads[5].wait()
     lower(0, True)
@@ -491,6 +531,7 @@
         )
 
     halves = [None, None]
+    backs = {}
     for rel in (1, 0):
         incoming_hidden(rel).wait_recv()
         lower(rel, False)
@@ -498,8 +539,6 @@
         halves[rel] = send(
             half_out.at[rel], half_in.at[rel], half_send.at[rel], half_recv.at[rel], core_partner
         )
-    backs = {}
-    for rel in (1, 0):
         halves[rel].wait_recv()
         total = (expert_sum[rel, :cap_rows, :] + half_in[rel].astype(jnp.float32)).astype(jnp.bfloat16)
         chosen = placer[rel * zs * block : (rel + 1) * zs * block, rel * cap_rows : (rel + 1) * cap_rows]
@@ -529,15 +568,16 @@
         return total
 
     last_out[...] = mix(1).astype(jnp.bfloat16)
-    last = send(last_out, last_in, one_send.at[4], one_recv.at[4], ctx_partner)
+    last = send(last_out, last_in, one_send.at[1], one_recv.at[1], ctx_partner)
     near = pl.ds(pl.multiple_of(ctx * columns, 128), columns)
     far = pl.ds(pl.multiple_of(other_ctx * columns, 128), columns)
     mixed[:, near] = (resid[:, near] + mix(0)).astype(jnp.bfloat16)
     last.wait_recv()
     mixed[:, far] = (resid[:, far] + last_in[...].astype(jnp.float32)).astype(jnp.bfloat16)
 
-    sent += [state_copy, hidden_near, hidden_far, passed, last]
-    for copy in sent + infos + pairs + projected + gathers + halves + list(backs.values()):
+    sent += [state_copy, hidden_near, hidden_far, last] + to_ctx + to_core + passed
+    sent += sum(gathers, [])
+    for copy in sent + infos + pairs + projected + halves + list(backs.values()):
         copy.wait_send()
 
 
@@ -607,14 +647,20 @@
             dma((6,)),
             dma((2 * zs,)),
             dma((2 * zs,)),
-            dma((5,)),
-            dma((5,)),
+            dma((2,)),
+            dma((2,)),
             dma((PROJ_TILES,)),
             dma((PROJ_TILES,)),
             dma((PROJ_TILES * zs,)),
             dma((PROJ_TILES * zs,)),
-            dma((zs,)),
-            dma((zs,)),
+            dma((PROJ_TILES * zs,)),
+            dma((PROJ_TILES * zs,)),
+            dma((PROJ_TILES,)),
+            dma((PROJ_TILES,)),
+            dma((PROJ_TILES,)),
+            dma((PROJ_TILES,)),
+            dma((PROJ_TILES,)),
+            dma((PROJ_TILES,)),
             dma((2,)),
             dma((2,)),
             dma((2,)),
@@ -638,8 +684,8 @@
         attn_gain.reshape(1, -1),
         out_proj,
         moe_gain.reshape(1, -1),
-        routes,
-        route_weight,
+        routes.T,
+        route_weight.T,
         w_gate,
         w_up,
         w_down,

time: 68.5 us -> 62.1 us (0.907)
  Pallas kernels: 64.1 us -> 60.4 us
  local copies, waits for them, and re-layouts: 4.24 us -> 1.54 us
    pallas_call x1, Pallas kernels: 64.1 us -> 60.4 us  [per_device_kernel(): pl.pallas_call(functools.partial(layer_kernel, zs, capacity), out_shape=j...]
    unnamed x3 -> x1, local copies, waits for them, and re-layouts: 4.24 us -> 1.54 us
where the time goes in v2:
time: 62.1 us; the launch traced here: 62 us
  Pallas kernels  60.4 us (97%)
  local copies, waits for them, and re-layouts  1.54 us (2%)
    pallas_call x1, Pallas kernels, per_device_kernel(): pl.pallas_call(functools.partial(layer_kernel, zs, capacity), out_shape=j...  60.4 us
    unnamed x1, local copies, waits for them, and re-layouts  1.54 us

profile of v2, /device:TPU:0, one launch (start us, length us, event | category | flops | bytes accessed | tf_op | source)
XLA Modules:
  0.0 62.0 jit_solution(3136547077241492395)
XLA Ops:
  0.0 60.4 %shard_map.136 = bf16[16,3072]{1,0:T(8,128)(2,1)} custom-call(bf16[16,3072]{1,0:T(8,128)(2,1)} %resid_in.1, bf16[128,256]{1,0:T(8,128)(2,1)} %queries.1, bf16[128,256]{1,0:T(8,128)(2,1)} %keys.1, bf16[128,256]{1,0:T(8,128)(2,1)} %values.1, bf16[128,256]{1,0:T(8,128)(2,1)} %out_gate.1, f32[2,128]{1,0:T(2,128)} %log_decay.1, f32[1,256]{1,0:T(1,128)} %bitcast.5, ...), custom_call_target="tpu_custom_call" | custom-call | flops 4076863488 | bytes 21233664 | tf_op jit(solution)/shard_map/pallas_call | solution.py:616
  60.4 1.5 %copy.16 = bf16[16,3072]{1,0:T(8,128)(2,1)} copy(bf16[16,3072]{1,0:T(8,128)(2,1)} %shard_map.136) | data formatting | bytes 196608

commit v3 on v2

--- a/solution.py
+++ b/solution.py
@@ -472,6 +472,20 @@
     def activate(gate_part, up_part):
         return (jax.nn.silu(gate_part) * up_part).astype(jnp.bfloat16)
 
+    early = whole // WIDE // 2
+    hidden_cuts = [(0, early * WIDE), (early * WIDE, half - early * WIDE)]
+
+    def exchange_hidden(rel, part):
+        span = pl.ds(*hidden_cuts[part])
+        return pltpu.make_async_remote_copy(
+            src_ref=hidden_own.at[rel, :, span],
+            dst_ref=hidden_in.at[1 - rel, :, span],
+            send_sem=hidden_send.at[2 * rel + part],
+            recv_sem=hidden_recv.at[2 * (1 - rel) + part],
+            device_id=ctx_partner,
+            device_id_type=MESH,
+        )
+
     def hide(rel):
         def step(n, carry):
             span = pl.ds(pl.multiple_of(n * WIDE, WIDE), WIDE)
@@ -481,25 +495,25 @@
             )
             return carry
 
-        lax.fori_loop(0, whole // WIDE, step, 0)
+        lax.fori_loop(0, early, step, 0)
+        copies = [exchange_hidden(rel, 0)]
+        copies[0].start()
+        lax.fori_loop(early, whole // WIDE, step, 0)
         both = dot32(picked[rel].reshape(2 * cap_rows, width), w_rest[...])
         hidden_own[rel, :, whole:] = activate(both[:, :rest], both[:, rest:])
-        return send(
-            hidden_own.at[rel],
-            hidden_in.at[1 - rel],
-            hidden_send.at[rel],
-            hidden_recv.at[1 - rel],
-            ctx_partner,
-        )
-
-    def lower(rel, first):
+        copies.append(exchange_hidden(rel, 1))
+        copies[1].start()
+        return copies
+
+    def lower(rel, first, start, size, tiles):
         source = hidden_own if first else hidden_in
         side = ctx if first else other_ctx
 
         def step(n, carry):
             span = pl.ds(pl.multiple_of(n * WIDE, WIDE), WIDE)
             product = dot32(
-                source[rel], w_down[pl.ds(pl.multiple_of(side * half, 128), half), span]
+                source[rel, :, start : start + size],
+                w_down[pl.ds(pl.multiple_of(side * half + start, 128), size), span],
             )
             if first:
                 expert_sum[rel, :, span] = product
@@ -507,7 +521,7 @@
                 expert_sum[rel, :, span] += product
             return carry
 
-        lax.fori_loop(0, columns // WIDE, step, 0)
+        lax.fori_loop(tiles[0], tiles[1], step, 0)
 
     for load in loads[1:5]:
         load.wait()
@@ -517,49 +531,55 @@
         copy.wait_recv()
     hidden_far = hide(1)
     loads[5].wait()
-    lower(0, True)
-    lower(1, True)
-
-    def incoming_hidden(rel):
-        return pltpu.make_async_remote_copy(
-            src_ref=hidden_own.at[1 - rel],
-            dst_ref=hidden_in.at[rel],
-            send_sem=hidden_send.at[1 - rel],
-            recv_sem=hidden_recv.at[rel],
-            device_id=ctx_partner,
-            device_id_type=MESH,
-        )
-
-    halves = [None, None]
+    all_tiles = (0, columns // WIDE)
+    middle = columns // WIDE // 2
+    lower(0, True, 0, half, all_tiles)
+    lower(1, True, 0, half, all_tiles)
+    tile_cuts = [(0, middle), (middle, columns // WIDE)]
+
+    halves = []
     backs = {}
     for rel in (1, 0):
-        incoming_hidden(rel).wait_recv()
-        lower(rel, False)
-        half_out[rel] = expert_sum[rel, cap_rows:, :].astype(jnp.bfloat16)
-        halves[rel] = send(
-            half_out.at[rel], half_in.at[rel], half_send.at[rel], half_recv.at[rel], core_partner
-        )
-        halves[rel].wait_recv()
-        total = (expert_sum[rel, :cap_rows, :] + half_in[rel].astype(jnp.float32)).astype(jnp.bfloat16)
+        exchange_hidden(1 - rel, 0).wait_recv()
+        lower(rel, False, *hidden_cuts[0], all_tiles)
+        exchange_hidden(1 - rel, 1).wait_recv()
+        for part in range(2):
+            lower(rel, False, *hidden_cuts[1], tile_cuts[part])
+            span = slice(tile_cuts[part][0] * WIDE, tile_cuts[part][1] * WIDE)
+            half_out[rel, :, span] = expert_sum[rel, cap_rows:, span].astype(jnp.bfloat16)
+            halves.append(
+                send(
+                    half_out.at[rel, :, span],
+                    half_in.at[rel, :, span],
+                    half_send.at[2 * rel + part],
+                    half_recv.at[2 * rel + part],
+                    core_partner,
+                )
+            )
         chosen = placer[rel * zs * block : (rel + 1) * zs * block, rel * cap_rows : (rel + 1) * cap_rows]
-        spread_rows = dot32(chosen, total).astype(jnp.bfloat16)
-        back_in[rel, 0] = spread_rows[:block]
-        for d in range(1, zs):
-            back_out[rel, d] = spread_rows[d * block : (d + 1) * block]
-            backs[rel, d] = send(
-                back_out.at[rel, d],
-                back_in.at[rel, d],
-                back_send.at[rel * zs + d],
-                back_recv.at[rel * zs + d],
-                device(ctx, behind(d), core),
-            )
+        for part in range(2):
+            span = slice(tile_cuts[part][0] * WIDE, tile_cuts[part][1] * WIDE)
+            halves[part - 2].wait_recv()
+            total = expert_sum[rel, :cap_rows, span] + half_in[rel, :, span].astype(jnp.float32)
+            spread_rows = dot32(chosen, total.astype(jnp.bfloat16)).astype(jnp.bfloat16)
+            back_in[rel, 0, :, span] = spread_rows[:block]
+            for d in range(1, zs):
+                back_out[rel, d, :, span] = spread_rows[d * block : (d + 1) * block]
+                backs[rel, d, part] = send(
+                    back_out.at[rel, d, :, span],
+                    back_in.at[rel, d, :, span],
+                    back_send.at[(2 * rel + part) * zs + d],
+                    back_recv.at[(2 * rel + part) * zs + d],
+                    device(ctx, behind(d), core),
+                )
 
     def mix(rel):
         table = info[rel, 0]
         total = jnp.zeros((block, columns), jnp.float32)
         for d in range(zs):
             if d:
-                backs[rel, d].wait_recv()
+                backs[rel, d, 0].wait_recv()
+                backs[rel, d, 1].wait_recv()
             expert = ahead(d).astype(jnp.float32)
             weight = jnp.where(table[:, 0:1] == expert, table[:, 2:3], 0.0) + jnp.where(
                 table[:, 1:2] == expert, table[:, 3:4], 0.0
@@ -575,7 +595,7 @@
     last.wait_recv()
     mixed[:, far] = (resid[:, far] + last_in[...].astype(jnp.float32)).astype(jnp.bfloat16)
 
-    sent += [state_copy, hidden_near, hidden_far, last] + to_ctx + to_core + passed
+    sent += [state_copy, last] + hidden_near + hidden_far + to_ctx + to_core + passed
     sent += sum(gathers, [])
     for copy in sent + infos + pairs + projected + halves + list(backs.values()):
         copy.wait_send()
@@ -661,12 +681,12 @@
             dma((PROJ_TILES,)),
             dma((PROJ_TILES,)),
             dma((PROJ_TILES,)),
-            dma((2,)),
-            dma((2,)),
-            dma((2,)),
-            dma((2,)),
-            dma((2 * zs,)),
-            dma((2 * zs,)),
+            dma((4,)),
+            dma((4,)),
+            dma((4,)),
+            dma((4,)),
+            dma((4 * zs,)),
+            dma((4 * zs,)),
         ],
         compiler_params=pltpu.CompilerParams(
             collective_id=0, has_side_effects=True, vmem_limit_bytes=56 * 1024 * 1024

time: 62.1 us -> 63 us (1.014)
  Pallas kernels: 60.4 us -> 61.2 us
    pallas_call x1, Pallas kernels: 60.4 us -> 61.2 us  [per_device_kernel(): pl.pallas_call(functools.partial(layer_kernel, zs, capacity), out_shape=j...]
where the time goes in v3:
time: 63 us; the launch traced here: 62.8 us
  Pallas kernels  61.2 us (97%)
  local copies, waits for them, and re-layouts  1.54 us (2%)
    pallas_call x1, Pallas kernels, per_device_kernel(): pl.pallas_call(functools.partial(layer_kernel, zs, capacity), out_shape=j...  61.2 us
    unnamed x1, local copies, waits for them, and re-layouts  1.54 us

profile of v3, /device:TPU:0, one launch (start us, length us, event | category | flops | bytes accessed | tf_op | source)
XLA Modules:
  0.0 62.8 jit_solution(15016425644859485106)
XLA Ops:
  0.0 61.2 %shard_map.136 = bf16[16,3072]{1,0:T(8,128)(2,1)} custom-call(bf16[16,3072]{1,0:T(8,128)(2,1)} %resid_in.1, bf16[128,256]{1,0:T(8,128)(2,1)} %queries.1, bf16[128,256]{1,0:T(8,128)(2,1)} %keys.1, bf16[128,256]{1,0:T(8,128)(2,1)} %values.1, bf16[128,256]{1,0:T(8,128)(2,1)} %out_gate.1, f32[2,128]{1,0:T(2,128)} %log_decay.1, f32[1,256]{1,0:T(1,128)} %bitcast.5, ...), custom_call_target="tpu_custom_call" | custom-call | flops 4076863488 | bytes 21233664 | tf_op jit(solution)/shard_map/pallas_call | solution.py:636
  61.2 1.5 %copy.16 = bf16[16,3072]{1,0:T(8,128)(2,1)} copy(bf16[16,3072]{1,0:T(8,128)(2,1)} %shard_map.136) | data formatting | bytes 196608

commit v4 on v2

--- a/solution.py
+++ b/solution.py
@@ -145,7 +145,7 @@
 
 
 MESH = pl.DeviceIdType.MESH
-PROJ_TILES = 3
+PROJ_TILES = 6
 WIDE = 256
 
 
@@ -492,19 +492,23 @@
             ctx_partner,
         )
 
-    def lower(rel, first):
-        source = hidden_own if first else hidden_in
-        side = ctx if first else other_ctx
-
+    def lower_own():
         def step(n, carry):
             span = pl.ds(pl.multiple_of(n * WIDE, WIDE), WIDE)
-            product = dot32(
-                source[rel], w_down[pl.ds(pl.multiple_of(side * half, 128), half), span]
+            expert_sum[:, :, span] = dot32(
+                hidden_own[...].reshape(4 * cap_rows, half),
+                w_down[pl.ds(pl.multiple_of(ctx * half, 128), half), span],
+            ).reshape(2, 2 * cap_rows, WIDE)
+            return carry
+
+        lax.fori_loop(0, columns // WIDE, step, 0)
+
+    def lower(rel):
+        def step(n, carry):
+            span = pl.ds(pl.multiple_of(n * WIDE, WIDE), WIDE)
+            expert_sum[rel, :, span] += dot32(
+                hidden_in[rel], w_down[pl.ds(pl.multiple_of(other_ctx * half, 128), half), span]
             )
-            if first:
-                expert_sum[rel, :, span] = product
-            else:
-                expert_sum[rel, :, span] += product
             return carry
 
         lax.fori_loop(0, columns // WIDE, step, 0)
@@ -517,8 +521,7 @@
         copy.wait_recv()
     hidden_far = hide(1)
     loads[5].wait()
-    lower(0, True)
-    lower(1, True)
+    lower_own()
 
     def incoming_hidden(rel):
         return pltpu.make_async_remote_copy(
@@ -534,7 +537,7 @@
     backs = {}
     for rel in (1, 0):
         incoming_hidden(rel).wait_recv()
-        lower(rel, False)
+        lower(rel)
         half_out[rel] = expert_sum[rel, cap_rows:, :].astype(jnp.bfloat16)
         halves[rel] = send(
             half_out.at[rel], half_in.at[rel], half_send.at[rel], half_recv.at[rel], core_partner

time: 62.1 us -> 61.7 us (level)
  no operation moved by 1% of the time
where the time goes in v4:
time: 61.7 us; the launch traced here: 61.5 us
  Pallas kernels  60 us (97%)
  local copies, waits for them, and re-layouts  1.54 us (2%)
    pallas_call x1, Pallas kernels, per_device_kernel(): pl.pallas_call(functools.partial(layer_kernel, zs, capacity), out_shape=j...  60 us
    unnamed x1, local copies, waits for them, and re-layouts  1.54 us

profile of v4, /device:TPU:0, one launch (start us, length us, event | category | flops | bytes accessed | tf_op | source)
XLA Modules:
  0.0 61.5 jit_solution(10022749669949558129)
XLA Ops:
  0.0 60.0 %shard_map.136 = bf16[16,3072]{1,0:T(8,128)(2,1)} custom-call(bf16[16,3072]{1,0:T(8,128)(2,1)} %resid_in.1, bf16[128,256]{1,0:T(8,128)(2,1)} %queries.1, bf16[128,256]{1,0:T(8,128)(2,1)} %keys.1, bf16[128,256]{1,0:T(8,128)(2,1)} %values.1, bf16[128,256]{1,0:T(8,128)(2,1)} %out_gate.1, f32[2,128]{1,0:T(2,128)} %log_decay.1, f32[1,256]{1,0:T(1,128)} %bitcast.5, ...), custom_call_target="tpu_custom_call" | custom-call | flops 4076863488 | bytes 21233664 | tf_op jit(solution)/shard_map/pallas_call | solution.py:619
  60.0 1.5 %copy.16 = bf16[16,3072]{1,0:T(8,128)(2,1)} copy(bf16[16,3072]{1,0:T(8,128)(2,1)} %shard_map.136) | data formatting | bytes 196608
